TPU v7x, 128 devices: a whole 4x4x4 slice. The times are simulated.
128 devices in a mesh: dp: 16 (over x, y), neg: 8 (over z, core).
Axes of the slice: x: 4, y: 4, z: 4, core: 2. Of those that a mesh axis runs over, the one named last changes fastest.
Arguments:
- queries: bfloat16 [8192, 4096], P('dp'), may hold values from -144 to 144, as said below
- passages: bfloat16 [32768, 4096], P(('dp', 'neg')), may hold values from -6 to 6
- list_owner: int32 [8, 2048, 1], P('neg', 'dp'), may hold values from 0 to 127; in each aligned block of 128 rows (0 to 127, 128 to 255, ..., all dimensions but the last counted through in order) at most 2 rows name the same one
- list_row: int32 [8, 2048], P('neg', 'dp'), may hold values from 0 to 255
- positive: int32 [8192], P('dp'), may hold values from 0 to 16383
- row_weight: float32 [8192], P('dp'), may hold values from 8 to 32
Outputs:
- query_grad: bfloat16 [8192, 4096], P('dp', 'neg')
- passage_grad: float32 [32768, 4096], P(('dp', 'neg'))
Inputs may be any that keep to these rules, and one draw needn't show every extreme that they name: `queries`: queries are embedding activations. `list_owner`: among the 128 entries of one device no owner appears more than 2 times, and in every draw some device names some owner exactly 2 times.
All inputs are finite; a program needn't handle non-finite values.
Results may differ from a plain program's by a relative error of at most 0.015.
Values may be sent and summed in bfloat16 or wider, within the bound.
A program may use at most 192 MiB of HBM per device.

v0:
```python
import math

import jax
import jax.numpy as jnp
from jax import lax
from jax.sharding import PartitionSpec as P


def body(queries, passages, list_owner, list_row, positive, row_weight):
    owners = list_owner.reshape(-1)
    row_ids = list_row.reshape(-1)
    list_len = owners.shape[0]
    width = queries.shape[1]
    dp_size = lax.axis_size("dp")
    neg_size = lax.axis_size("neg")
    devices = dp_size * neg_size
    capacity = max(2, 2 * list_len // devices)
    slot_count = devices * capacity
    entry = jnp.arange(list_len, dtype=jnp.int32)
    same_owner = owners[:, None] == owners[None, :]
    earlier = entry[:, None] > entry[None, :]
    slot_rank = jnp.sum((same_owner & earlier).astype(jnp.int32), axis=1)
    slot_index = owners * capacity + slot_rank
    place_table = jnp.arange(slot_count, dtype=jnp.int32)[:, None] == slot_index[None, :]
    place_bf = place_table.astype(jnp.bfloat16)
    requests = jnp.sum(jnp.where(place_table, row_ids[None, :] + 1, 0), axis=1)
    asked_rows = lax.all_to_all(
        requests.reshape(devices, capacity), ("dp", "neg"), split_axis=0, concat_axis=0, tiled=True
    )
    asked_rows = asked_rows.reshape(-1)
    pass_rows = passages.shape[0]
    pick_table = (
        asked_rows[:, None] - 1 == jnp.arange(pass_rows, dtype=jnp.int32)[None, :]
    ).astype(jnp.bfloat16)
    outgoing = jnp.dot(pick_table, passages, preferred_element_type=jnp.float32).astype(
        jnp.bfloat16
    )
    incoming = lax.all_to_all(
        outgoing.reshape(devices, capacity, width),
        ("dp", "neg"),
        split_axis=0,
        concat_axis=0,
        tiled=True,
    )
    incoming = incoming.reshape(slot_count, width)
    own_rows = lax.dot_general(
        place_bf, incoming, (((0,), (0,)), ((), ())), preferred_element_type=jnp.float32
    ).astype(jnp.bfloat16)
    column_block = lax.all_gather(own_rows, "dp", axis=0, tiled=True)
    block_rows = column_block.shape[0]
    logit_scale = 3.0 / math.sqrt(width)
    logits = (
        lax.dot_general(
            queries, column_block, (((1,), (1,)), ((), ())), preferred_element_type=jnp.float32
        )
        * logit_scale
    )
    local_max = jnp.max(logits, axis=1)
    local_sum = jnp.sum(jnp.exp(logits - local_max[:, None]), axis=1)
    row_max = lax.pmax(local_max, "neg")
    row_total = lax.psum(local_sum * jnp.exp(local_max - row_max), "neg")
    probability = jnp.exp(logits - row_max[:, None]) / row_total[:, None]
    first_col = lax.axis_index("neg") * block_rows
    target = (
        positive[:, None] == first_col + jnp.arange(block_rows, dtype=jnp.int32)[None, :]
    ).astype(jnp.float32)
    logit_grad = (row_weight[:, None] * logit_scale * (probability - target)).astype(jnp.bfloat16)
    partial_value = jnp.dot(logit_grad, column_block, preferred_element_type=jnp.float32)
    query_grad = lax.psum_scatter(
        partial_value.astype(jnp.bfloat16), "neg", scatter_dimension=1, tiled=True
    )
    column_grad = lax.psum_scatter(
        lax.dot_general(
            logit_grad, queries, (((0,), (0,)), ((), ())), preferred_element_type=jnp.float32
        ).astype(jnp.bfloat16),
        "dp",
        scatter_dimension=0,
        tiled=True,
    ).astype(jnp.float32)
    slot_entry = jnp.sum(jnp.where(place_table, entry[None, :] + 1, 0), axis=1) - 1
    send_slots = jnp.where((slot_entry >= 0)[:, None], column_grad[jnp.maximum(slot_entry, 0)], 0.0)
    returned = lax.all_to_all(
        send_slots.reshape(devices, capacity, width).astype(jnp.bfloat16),
        ("dp", "neg"),
        split_axis=0,
        concat_axis=0,
        tiled=True,
    ).astype(jnp.float32)
    returned = returned.reshape(slot_count, width)
    passage_grad = lax.dot_general(
        pick_table.astype(jnp.float32),
        returned,
        (((0,), (0,)), ((), ())),
        precision=lax.Precision.HIGHEST,
        preferred_element_type=jnp.float32,
    )
    return (query_grad, passage_grad)


def solution(mesh):
    in_specs = (
        P("dp", None),
        P(("dp", "neg"), None),
        P("neg", "dp", None),
        P("neg", "dp"),
        P("dp"),
        P("dp"),
    )
    out_specs = (P("dp", "neg"), P(("dp", "neg"), None))
    return jax.shard_map(body, mesh=mesh, in_specs=in_specs, out_specs=out_specs, check_vma=False)
```

profile of v0, /device:TPU:1, one launch (start us, length us, event | category | flops | bytes accessed | tf_op | source)
XLA Modules:
  0.0 418.0 jit_solution(18103486923802859172)
XLA Ops:
  7.2 0.0 all-gather.2.cloned.1.call-start
  7.2 1.0 convert_reduce_fusion
  8.2 0.7 iota_add_fusion.1
  8.9 0.7 add_bitcast_fusion
  9.5 0.1 select_reduce_fusion
  9.7 0.1 all_to_all.12
  9.8 20.7 %all_to_all.19 = s32[128,1,2]{2,1,0:T(1,128)S(1)} all-to-all(s32[128,1,2]{2,1,0:T(1,128)S(1)} %bitcast.20), channel_id=1, replica_groups=mesh['dp'=16,'neg'=8] {'dp','neg'}, dimensions={0} | all-to-all | bytes 2048 | tf_op jit(solution)/shard_map/all_to_all | solution.py:27
  30.5 0.2 add_reduce_fusion
  30.7 0.1 sub.35
  30.8 2.1 convolution_convert_fusion.2
  32.9 3.2 reshape.86
  36.1 35.3 %all_to_all.20 = bf16[128,2,4096]{2,1,0:T(2,128)(2,1)} all-to-all(bf16[128,2,4096]{2,1,0:T(2,128)(2,1)S(1)} %reshape.86), channel_id=1, replica_groups=mesh['dp'=16,'neg'=8] {'dp','neg'}, dimensions={0} | all-to-all | bytes 4194304 | tf_op jit(solution)/shard_map/all_to_all | solution.py:38
  71.4 2.8 reshape.87
  74.2 1.5 convolution_convert_fusion.3
  75.7 0.0 reduce-scatter.5.cloned.1.call-start
  75.8 107.1 %all-gather.2.cloned.1.call-done = bf16[2048,4096]{1,0:T(8,128)(2,1)} async-done(((bf16[128,4096]{1,0:T(8,128)(2,1)}), bf16[2048,4096]{1,0:T(8,128)(2,1)}) %all-gather.2.cloned.1.call-update) | async-done | bytes 16777232 | tf_op jit(solution)/shard_map/all_gather | solution.py:49
  182.9 15.0 %multiply_reduce_fusion = (f32[512]{0:T(512)S(1)}, f32[2048,512]{1,0:T(8,128)}) fusion(bf16[2048,4096]{1,0:T(8,128)(2,1)} %all-gather.2.cloned.1.call-done, bf16[512,4096]{1,0:T(8,128)(2,1)} %param.6), kind=kOutput, calls=%fused_computation.10 | convolution fusion | flops 8592031744 | bytes 25167872 | tf_op jit(solution)/shard_map/dot_general | solution.py:53
  197.8 12.7 %pmax.7 = f32[512]{0:T(512)S(1)} all-reduce(f32[512]{0:T(512)S(1)} %get-tuple-element.4), channel_id=1, replica_groups=mesh['dp'=16,'neg'=8] {'neg'}, use_global_device_ids=true, to_apply=%region_3.4 | all-reduce | flops 512 | bytes 4096 | tf_op jit(solution)/shard_map/pmax | solution.py:60
  210.5 2.9 exponential_reduce_fusion
  213.5 14.8 %psum.7 = f32[512]{0:T(512)S(1)} all-reduce(f32[512]{0:T(512)S(1)} %exponential_multiply_fusion), channel_id=1, replica_groups=mesh['dp'=16,'neg'=8] {'neg'}, use_global_device_ids=true, to_apply=%region_5.6 | all-reduce | flops 512 | bytes 4096 | tf_op jit(solution)/shard_map/psum | solution.py:61
  228.3 15.7 %convolution_convert_fusion = bf16[2048,4096]{1,0:T(8,128)(2,1)} fusion(bf16[512,4096]{1,0:T(8,128)(2,1)} %param.6, f32[2048,512]{1,0:T(8,128)} %get-tuple-element.5, s32[512]{0:T(512)S(1)} %copy-done.3, f32[512]{0:T(512)S(1)} %psum.7, f32[512]{0:T(512)S(1)} %pmax.7, f32[512]{0:T(512)S(1)} %broadcast_multiply_fusion, s32[2048]{0:T(1024)S(1)} %iota_add_fusion), kind=kOutput, calls=%fused_computation.1 | convolution fusion | flops 8606711808 | bytes 25182208 | tf_op jit(solution)/shard_map/dot_general | solution.py:73
  244.0 0.0 reduce-scatter.3.cloned.1.call-start
  244.0 16.5 %convolution_convert_fusion.1 = bf16[512,4096]{1,0:T(8,128)(2,1)} fusion(bf16[2048,4096]{1,0:T(8,128)(2,1)} %all-gather.2.cloned.1.call-done, f32[2048,512]{1,0:T(8,128)} %get-tuple-element.5, s32[512]{0:T(512)S(1)} %copy-done.3, f32[512]{0:T(512)S(1)} %psum.7, f32[512]{0:T(512)S(1)} %pmax.7, f32[512]{0:T(512)S(1)} %broadcast_multiply_fusion, ...), kind=kOutput, calls=%fused_computation.2 | convolution fusion | flops 8600420352 | bytes 25182208 | tf_op jit(solution)/shard_map/dot_general | solution.py:68
  260.5 0.2 ge.11
  260.7 90.7 %reduce-scatter.5.cloned.1.call-done = bf16[128,4096]{1,0:T(8,128)(2,1)} async-done(((bf16[2048,4096]{1,0:T(8,128)(2,1)}), bf16[128,4096]{1,0:T(8,128)(2,1)}) %reduce-scatter.5.cloned.1.call-update) | async-done | bytes 1048592 | tf_op jit(solution)/shard_map/reduce_scatter | solution.py:72
  351.4 5.2 %gather_fusion = bf16[256,4096]{1,0:T(8,128)(2,1)S(1)} fusion(bf16[128,4096]{1,0:T(8,128)(2,1)} %reduce-scatter.5.cloned.1.call-done, s32[1024]{0:T(1024)S(1)} %pad_clamp_fusion), kind=kCustom, calls=%fused_computation | custom fusion | bytes 4195328 | tf_op jit(solution)/shard_map/gather | solution.py:81
  356.6 2.6 gather.6
  359.2 4.7 %select_convert_fusion = bf16[128,2,4096]{2,1,0:T(2,128)(2,1)S(1)} fusion(bf16[128,2,4096]{2,1,0:T(2,128)(2,1)} %gather.6, pred[128,2]{1,0:T(8,128)(4,1)S(1)} %ge.11), kind=kLoop, calls=%fused_computation.8 | loop fusion | flops 1048576 | bytes 4194560 | tf_op jit(solution)/shard_map/convert_element_type | solution.py:83
  363.9 38.7 %all_to_all.21 = bf16[128,2,4096]{2,1,0:T(2,128)(2,1)} all-to-all(bf16[128,2,4096]{2,1,0:T(2,128)(2,1)S(1)} %select_convert_fusion), channel_id=1, replica_groups=mesh['dp'=16,'neg'=8] {'dp','neg'}, dimensions={0} | all-to-all | bytes 4194304 | tf_op jit(solution)/shard_map/all_to_all | solution.py:82
  402.6 4.3 %reshape.88 = bf16[256,4096]{1,0:T(8,128)(2,1)} reshape(bf16[128,2,4096]{2,1,0:T(2,128)(2,1)} %all_to_all.21) | data formatting | bytes 4194304 | tf_op jit(solution)/shard_map/reshape | solution.py:89
  407.0 4.5 %fusion.2 = f32[256,4096]{1,0:T(8,128)} fusion(bf16[256,4096]{1,0:T(8,128)(2,1)} %reshape.88, s32[256]{0:T(256)S(1)} %sub.35), kind=kOutput, calls=%fused_computation.12 | convolution fusion | flops 536936448 | bytes 6292480 | tf_op jit(solution)/shard_map/dot_general | solution.py:90
  411.4 0.0 reduce-scatter.3.cloned.1.call-done
  (17 shorter events, 0.1 us)
Async XLA Ops:
  7.2 23.7 %copy-start = (bf16[256,4096]{1,0:T(8,128)(2,1)S(1)}, bf16[256,4096]{1,0:T(8,128)(2,1)}, u32[]{:S(2)}) copy-start(bf16[256,4096]{1,0:T(8,128)(2,1)} %param.7) | copy-start | bytes 6291460
  7.2 175.7 %all-gather.2.cloned.1.call-start = ((), (), s32[]{:S(2)}) async-start(), calls=%async_computation.5 | async-start | bytes 17825792 | tf_op jit(solution)/shard_map/all_gather | solution.py:49
  71.4 4.3 %copy-start.2 = (f32[512]{0:T(512)S(1)}, f32[512]{0:T(512)}, u32[]{:S(2)}) copy-start(f32[512]{0:T(512)} %param.11) | copy-start | bytes 6148
  75.7 275.7 %reduce-scatter.5.cloned.1.call-start = ((), (), s32[]{:S(2)}) async-start(), calls=%async_computation.7 | async-start | bytes 17825792 | tf_op jit(solution)/shard_map/reduce_scatter | solution.py:72
  197.8 30.5 %copy-start.3 = (s32[512]{0:T(512)S(1)}, s32[512]{0:T(512)}, u32[]{:S(2)}) copy-start(s32[512]{0:T(512)} %param.10) | copy-start | bytes 6148
  244.0 167.5 %reduce-scatter.3.cloned.1.call-start = ((), (), s32[]{:S(2)}) async-start(), calls=%async_computation.6 | async-start | bytes 4718592 | tf_op jit(solution)/shard_map/reduce_scatter | solution.py:69
  402.6 8.8 %copy-start.1 = (bf16[256,4096]{1,0:T(8,128)(2,1)S(1)}, bf16[256,4096]{1,0:T(8,128)(2,1)}, u32[]{:S(2)}) copy-start(bf16[256,4096]{1,0:T(8,128)(2,1)} %param.7) | copy-start | bytes 6291460
Sparse Core Ops, SparseCore 0:
  75.8 107.0 all-gather.1
  244.1 107.2 reduce-scatter.4
  354.3 57.0 reduce-scatter.2
where the time goes:
time: 421 us; the launch traced here: 418 us
  waiting for transfers between devices  198 us (47%)
  blocking collectives  122 us (29%)
  matrix products  55.1 us (13%)
  local copies, waits for them, and re-layouts  18.5 us (4%)
  between operations  13.9 us (3%)
  other arithmetic  10.3 us (2%)
    all_gather x1, waiting for transfers between devices, body(): column_block = lax.all_gather(own_rows, 'dp', axis=0, tiled=True)  107 us
    reduce_scatter x1, waiting for transfers between devices, body(): lax.psum_scatter(lax.dot_general(logit_grad, queries, (((0,), (0,)), ((),...  90.7 us
    all_to_all x1, blocking collectives, body(): lax.all_to_all(send_slots.reshape(devices, capacity, width).astype(jnp.bf...  38.7 us
    all_to_all x1, blocking collectives, body(): lax.all_to_all(outgoing.reshape(devices, capacity, width), ('dp', 'neg'),...  35.3 us
    all_to_all x1, blocking collectives, body(): lax.all_to_all(requests.reshape(devices, capacity), ('dp', 'neg'), split_...  20.7 us
    dot_general x1, matrix products, body(): jnp.dot(logit_grad, column_block, preferred_element_type=jnp.float32)  16.5 us
    dot_general x1, matrix products, body(): lax.dot_general(logit_grad, queries, (((0,), (0,)), ((), ())), preferred_...  15.7 us
    dot_general x1, matrix products, body(): lax.dot_general(queries, column_block, (((1,), (1,)), ((), ())), preferre...  15 us
  transfers between devices with their start and end apart: 3, of which 2 were waited for; matrix products, arithmetic and copies ran while one was open for 9% of the time, Pallas kernels for 0%

commit v1 on v0

v1 whole, which is shorter than its diff:
```python
import math

import jax
import jax.numpy as jnp
from jax import lax
from jax.experimental import pallas as pl
from jax.experimental.pallas import tpu as pltpu
from jax.sharding import PartitionSpec as P

MESH = pl.DeviceIdType.MESH
BF16 = jnp.bfloat16
F32 = jnp.float32
RING = 4
N_NEG = 8
LOW = -3.0e38

NN = (((1,), (0,)), ((), ()))
NT = (((1,), (1,)), ((), ()))
TN = (((0,), (0,)), ((), ()))


def dot(a, b, dims):
    return lax.dot_general(a, b, dims, preferred_element_type=F32)


class Sems:
    def __init__(self, ref):
        self.ref = ref
        self.used = 0

    def new(self):
        self.used += 1
        return self.ref.at[self.used - 1]


class RingScatter:
    def __init__(self, sems, right, left, view, first, second):
        self.view, self.first, self.second = view, first, second
        self.up, self.down = right, left
        self.sem = [(sems.new(), sems.new()) for _ in range(4)]
        self.copies = []

    def send(self, src, dst, index, to):
        copy = pltpu.make_async_remote_copy(
            src, dst, self.sem[index][0], self.sem[index][1], device_id=to, device_id_type=MESH
        )
        copy.start()
        self.copies.append(copy)
        return copy

    def start(self):
        self.a = self.send(self.view(2, 0), self.first.at[0], 0, self.up)
        self.b = self.send(self.view(2, 1), self.first.at[1], 1, self.down)

    def middle(self):
        self.a.wait_recv()
        self.b.wait_recv()
        part = self.view(1, 0)
        part[...] = (part[...].astype(F32) + self.first[0].astype(F32)).astype(BF16)
        self.c = self.send(self.view(1, None), self.second(0), 2, self.up)
        part = self.view(3, 1)
        part[...] = (part[...].astype(F32) + self.first[1].astype(F32)).astype(BF16)
        self.d = self.send(self.view(3, None), self.second(1), 3, self.down)

    def finish(self, dst):
        self.c.wait_recv()
        self.d.wait_recv()
        own = self.view(0, None)[...].astype(F32)
        dst[...] = (own + self.second(0)[...].astype(F32) + self.second(1)[...].astype(F32)).astype(BF16)

    def drain(self):
        for copy in self.copies:
            copy.wait_send()


def kernel(
    q_in, p_in, ids_in, pos_in, w_in,
    q_out, p_out, land,
    qv, pv, px, ev, gv, gx, pg, pg_first,
    ay1, az1, az2, bz1, by1, by2, q_res,
    ids, table, count, wp, m_b, s_b, st_own, st_in, st_mid, st_y, factor,
    sem_ref,
):
    dp, neg = lax.axis_index("dp"), lax.axis_index("neg")
    x, y = dp // RING, dp % RING
    z, core = neg // 2, neg % 2
    block, width = q_in.shape
    owned = p_in.shape[0]
    strip = width // N_NEG
    scale = 3.0 / math.sqrt(width)
    sems = Sems(sem_ref)

    def device(xx, yy, zz, cc):
        return ((xx % RING) * RING + yy % RING, (zz % RING) * 2 + cc)

    x_peer = [None] + [device(x + k, y, z, core) for k in (1, 2, 3)]
    y_peer = [None] + [device(x, y + k, z, core) for k in (1, 2, 3)]
    z_up, z_down = device(x, y, z + 1, core), device(x, y, z + 3, core)
    other = device(x, y, z, 1 - core)
    n_peer = [None] + [(dp, (neg + k) % N_NEG) for k in range(1, N_NEG)]

    barrier = pltpu.get_barrier_semaphore()
    greeted = x_peer[1:] + y_peer[1:] + n_peer[1:]
    for peer in greeted:
        pl.semaphore_signal(barrier, inc=1, device_id=peer, device_id_type=MESH)
    pl.semaphore_wait(barrier, len(greeted))

    sent = []

    def send(src, dst, to):
        copy = pltpu.make_async_remote_copy(
            src, dst, sems.new(), sems.new(), device_id=to, device_id_type=MESH
        )
        copy.start()
        sent.append(copy)
        return copy

    half = owned // 2
    lo, hi = pl.ds(0, half), pl.ds(half, half)
    p_right = [send(p_in.at[lo], pv.at[3, lo], x_peer[1])]
    p_left = [send(p_in.at[hi], pv.at[1, hi], x_peer[3])]
    piece = block // 8

    def rows(zz, cc, sub):
        return pl.ds(pl.multiple_of(zz * (4 * piece) + cc * (2 * piece) + sub * piece, piece), piece)

    zp = z % 2
    q_right = [send(q_in.at[rows(zp, core, 0)], qv.at[3, rows(zp, core, 0)], y_peer[1])]
    q_left = [send(q_in.at[rows(zp, core, 1)], qv.at[1, rows(zp, core, 1)], y_peer[3])]

    own_q = pltpu.make_async_copy(q_in, qv.at[0], sems.new())
    own_p = pltpu.make_async_copy(p_in, pv.at[0], sems.new())
    own_p.start()
    own_q.start()

    ids[dp, neg] = ids_in[0]
    copies = [send(ids.at[dp, neg], ids.at[dp, neg], n_peer[k]) for k in range(1, N_NEG)]
    p_right.append(send(p_in.at[hi], pv.at[3, hi], x_peer[1]))
    p_left.append(send(p_in.at[lo], pv.at[1, lo], x_peer[3]))
    q_right.append(send(q_in.at[rows(zp, core, 1)], qv.at[3, rows(zp, core, 1)], y_peer[1]))
    q_left.append(send(q_in.at[rows(zp, core, 0)], qv.at[1, rows(zp, core, 0)], y_peer[3]))
    for copy in copies:
        copy.wait_recv()
    copies = [send(ids.at[dp], ids.at[dp], y_peer[k]) for k in (1, 2, 3)]
    for copy in copies:
        copy.wait_recv()
    line = ids.at[pl.ds(x * RING, RING)]
    copies = [send(line, line, x_peer[k]) for k in (1, 2, 3)]
    for copy in copies:
        copy.wait_recv()

    lanes = ids.shape[-1]
    first_id = (dp * N_NEG + neg) * owned
    name = lax.broadcasted_iota(jnp.int32, (owned, lanes), 0) + first_id

    def tally(i, total):
        for j in range(N_NEG):
            total = total + jnp.where(name == ids[i, j], 1.0, 0.0)
        return total

    total = lax.fori_loop(0, RING * RING, tally, jnp.zeros((owned, lanes), F32))
    count[0] = dot(total.astype(BF16), jnp.ones((lanes, lanes), BF16), NN)
    counts = [send(count.at[0], count.at[4 - k], x_peer[k]) for k in (1, 2, 3)]

    for i in range(RING * RING):
        for j in range(N_NEG):
            table[pl.ds(i * N_NEG + j, 1), :] = ids[i, j]
    pos = pos_in[...]
    entry = jnp.bitwise_and(pos, lanes - 1)
    listing = jnp.bitwise_and(pos // lanes, RING * RING - 1) * N_NEG + pos // (lanes * RING * RING)
    side = lax.broadcasted_iota(jnp.int32, (lanes, block), 0)
    chosen = jnp.where(side == listing, 1.0, 0.0).astype(BF16)
    high = (table[...] // 256).astype(F32).astype(BF16)
    low = jnp.bitwise_and(table[...], 255).astype(F32).astype(BF16)
    found = dot(high, chosen, TN) * 256.0 + dot(low, chosen, TN)
    wp[0, 0:1, :] = w_in[...] * scale
    wp[0, 1:2, :] = jnp.sum(jnp.where(side == entry, found, 0.0), axis=0, keepdims=True)
    targets = [send(wp.at[0], wp.at[4 - k], y_peer[k]) for k in (1, 2, 3)]

    def logits(b, r):
        listed = count[b]
        listed = jnp.concatenate([listed] * (block // lanes), axis=1)
        value = dot(pv[b], qv[r], NT) * scale
        value = jnp.where(listed > 0.0, value, LOW)
        top = jnp.max(value, axis=0, keepdims=True)
        expo = jnp.exp(value - top) * listed
        place = pl.ds(pl.multiple_of(r * block, block), block)
        ev[b, :, place] = expo
        m_b[b, :, place] = top
        s_b[b, :, place] = jnp.sum(expo, axis=0, keepdims=True)

    own_p.wait()
    own_q.wait()
    logits(0, 0)

    from_z, from_core = {}, {}

    def pass_on(r, sub):
        view = qv.at[r, rows(zp, core, sub)]
        from_z[r, sub] = send(view, view, z_up if sub == 0 else z_down)
        from_core[r, 0, sub] = send(view, view, other)

    def pass_over(r, sub):
        from_z[r, sub].wait_recv()
        view = qv.at[r, rows(1 - zp, core, sub)]
        from_core[r, 1, sub] = send(view, view, other)

    def have(r):
        for key in from_core:
            if key[0] == r:
                from_core[key].wait_recv()

    def to_core(b):
        for k in range(RING):
            col = pl.ds(pl.multiple_of((((z + k) % RING) * 2 + 1 - core) * strip, strip), strip)
            crossed.append(send(pv.at[b, :, col], px.at[k, b], other))

    crossed = []
    to_core(0)
    q_right[0].wait_recv()
    q_far0 = send(qv.at[3, rows(zp, core, 0)], qv.at[2, rows(zp, core, 0)], y_peer[1])
    pass_on(3, 0)
    q_left[0].wait_recv()
    q_far1 = send(qv.at[1, rows(zp, core, 1)], qv.at[2, rows(zp, core, 1)], y_peer[3])
    pass_on(1, 1)
    p_right[0].wait_recv()
    p_far0 = send(pv.at[3, lo], pv.at[2, lo], x_peer[1])
    p_left[0].wait_recv()
    p_far1 = send(pv.at[1, hi], pv.at[2, hi], x_peer[3])
    q_right[1].wait_recv()
    pass_on(3, 1)
    q_left[1].wait_recv()
    pass_on(1, 0)
    pass_over(3, 0)
    pass_over(1, 1)
    q_far0.wait_recv()
    pass_on(2, 0)
    q_far1.wait_recv()
    pass_on(2, 1)
    pass_over(3, 1)
    pass_over(1, 0)
    have(1)
    have(3)
    pl.loop(0, 2)(lambda j: logits(0, 1 + 2 * j))
    for copy in counts + targets:
        copy.wait_recv()
    p_right[1].wait_recv()
    p_left[1].wait_recv()
    to_core(1)
    to_core(3)

    @pl.loop(0, 6)
    def _(i):
        j = i % 3
        logits(1 + 2 * (i // 3), j + j // 2)

    pass_over(2, 0)
    pass_over(2, 1)
    have(2)
    pl.loop(0, 3)(lambda i: logits(i + i // 2, 2))
    p_far0.wait_recv()
    p_far1.wait_recv()
    pl.loop(0, 4)(lambda r: logits(2, r))
    to_core(2)

    top = jnp.maximum(jnp.maximum(m_b[0], m_b[1]), jnp.maximum(m_b[2], m_b[3]))
    st_own[0:1, :] = top
    st_own[1:2, :] = sum(s_b[b] * jnp.exp(m_b[b] - top) for b in range(RING))
    copies = [send(st_own, st_in.at[k], n_peer[k]) for k in range(1, N_NEG)]
    for copy in copies:
        copy.wait_recv()
    for k in range(1, N_NEG):
        top = jnp.maximum(top, st_in[k, 0:1, :])
    mass = st_own[1:2, :] * jnp.exp(st_own[0:1, :] - top)
    for k in range(1, N_NEG):
        mass = mass + st_in[k, 1:2, :] * jnp.exp(st_in[k, 0:1, :] - top)
    st_mid[0:1, :] = top
    st_mid[1:2, :] = mass
    copies = [send(st_mid, st_y.at[k], y_peer[k]) for k in (1, 2, 3)]
    for copy in copies:
        copy.wait_recv()
    for r in range(RING):
        mine = pl.ds(r * block, block)
        theirs = [(k, pl.ds(((r + k) % RING) * block, block)) for k in (1, 2, 3)]
        top = st_mid[0:1, mine]
        for k, place in theirs:
            top = jnp.maximum(top, st_y[k, 0:1, place])
        mass = st_mid[1:2, mine] * jnp.exp(st_mid[0:1, mine] - top)
        for k, place in theirs:
            mass = mass + st_y[k, 1:2, place] * jnp.exp(st_y[k, 0:1, place] - top)
        weight = wp[r, 0:1, :] / mass
        for b in range(RING):
            factor[b, :, mine] = jnp.exp(m_b[b, :, mine] - top) * weight

    def gradient(b):
        base = ((((x + b) % RING) * RING + y) * N_NEG + neg) * owned
        label = (lax.broadcasted_iota(jnp.int32, (owned, block), 0) + base).astype(F32)
        for r in range(RING):
            place = pl.ds(r * block, block)
            hit = jnp.where(label == wp[r, 1:2, :], wp[r, 0:1, :], 0.0)
            gv[b, :, place] = (ev[b, :, place] * factor[b, :, place] - hit).astype(BF16)

    wide = width // 4

    def passage_part(b, n):
        col = pl.ds(pl.multiple_of(n * wide, wide), wide)
        return dot(gv[b], qv[:, :, col].reshape(RING * block, wide), NN)

    far = {}
    gradient(2)
    for n in (0, 2, 1, 3):
        col = pl.ds(n * wide, wide)
        pg[1, :, col] = passage_part(2, n).astype(BF16)
        far[n] = send(pg.at[1, :, col], pg_first.at[n], x_peer[1] if n < 2 else x_peer[3])
    grads = [send(gv.at[2], gx.at[2], other)]
    for b in (1, 3, 0):
        gradient(b)
        grads.append(send(gv.at[b], gx.at[b], other))

    @pl.loop(0, 8)
    def _(i):
        b = 1 + 2 * (i // 4)
        col = pl.ds(pl.multiple_of((i % 4) * wide, wide), wide)
        pg[b - 1, :, col] = passage_part(b, i % 4).astype(BF16)

    @pl.loop(0, 4)
    def _(n):
        col = pl.ds(pl.multiple_of((n % 2) * wide, wide), wide)
        ev[n // 2, :, col] = passage_part(0, n)

    near = {}
    before = len(sent)
    for n in (2, 3, 0, 1):
        col = pl.ds(n * wide, wide)
        b = 1 if n >= 2 else 3
        near[b, n] = send(pg.at[b - 1, :, col], land.at[0 if b == 1 else 1, n], x_peer[b])
    for n in (0, 1, 2, 3):
        col = pl.ds(n * wide, wide)
        b = 1 if n < 2 else 3
        far[n].wait_recv()
        pg[b - 1, :, col] = (pg[b - 1, :, col].astype(F32) + pg_first[n].astype(F32)).astype(BF16)
        near[b, n] = send(pg.at[b - 1, :, col], land.at[0 if b == 1 else 1, n], x_peer[b])

    for copy in sent[:before]:
        copy.wait_send()
    for copy in grads + crossed:
        copy.wait_recv()

    def query_part(r):
        place = pl.ds(pl.multiple_of(r * block, block), block)

        @pl.loop(0, RING)
        def _(k):
            col = pl.ds(pl.multiple_of((((z + k) % RING) * 2 + core) * strip, strip), strip)
            mine = dot(
                gv[:, :, place].reshape(RING * owned, block),
                pv[:, :, col].reshape(RING * owned, strip),
                TN,
            )
            theirs = dot(
                gx[:, :, place].reshape(RING * owned, block),
                px[k].reshape(RING * owned, strip),
                TN,
            )
            out = pl.ds(pl.multiple_of(k * strip, strip), strip)
            qv[r, :, out] = (mine + theirs).astype(BF16)

    mid = block // 2
    quarter = mid // 2

    def upper(rel, part):
        at = pl.ds(0, mid) if part is None else pl.ds(part * quarter, quarter)
        return qv.at[rel, at, pl.ds(0, RING * strip)]

    def lower(rel, part):
        at = pl.ds(mid, mid) if part is None else pl.ds(mid + part * quarter, quarter)
        return qv.at[rel, at, pl.ds(0, strip)]

    def across(r, start):
        def view(rel, part):
            at = pl.ds(start, mid) if part is None else pl.ds(start + part * quarter, quarter)
            return qv.at[r, at, pl.ds(rel * strip, strip)]

        return view

    def spare_upper(way):
        return qv.at[way, pl.ds(0, mid), pl.ds(RING * strip, RING * strip)]

    def spare_lower(r):
        return lambda way: qv.at[r, pl.ds(mid, mid), pl.ds((RING + way) * strip, strip)]

    def slots(ref):
        return lambda way: ref.at[way]

    a_y = RingScatter(sems, y_peer[1], y_peer[3], upper, ay1, spare_upper)
    a_z = RingScatter(sems, z_up, z_down, across(0, 0), az1, slots(az2))
    b_y = RingScatter(sems, y_peer[1], y_peer[3], lower, by1, slots(by2))
    b_z = {
        r: RingScatter(sems, z_up, z_down, across(r, mid), bz1.at[r], spare_lower(r)) for r in range(RING)
    }

    query_part(2)
    a_y.start()
    b_z[2].start()
    query_part(1)
    b_z[1].start()
    query_part(3)
    b_z[3].start()
    b_z[2].middle()
    a_y.middle()
    query_part(0)
    b_z[0].start()
    b_z[1].middle()
    b_z[3].middle()
    b_z[2].finish(lower(2, None))
    b_y.start()
    b_z[0].middle()
    b_z[1].finish(lower(1, None))
    b_z[3].finish(lower(3, None))
    b_y.middle()
    b_z[0].finish(lower(0, None))
    a_y.finish(upper(0, None))
    a_z.start()
    a_z.middle()
    b_y.finish(q_res.at[pl.ds(mid, mid)])
    a_z.finish(q_res.at[pl.ds(0, mid)])
    q_copy = pltpu.make_async_copy(q_res, q_out, sems.new())
    q_copy.start()

    loads, stores = {}, []
    for n in (0, 3, 1, 2):
        col = pl.ds(n * wide, wide)
        for b in (1, 3):
            near[b, n].wait()
            loads[b, n] = pltpu.make_async_copy(land.at[0 if b == 1 else 1, n], pg.at[b - 1, :, col], sems.new())
            loads[b, n].start()
    for n in (0, 3, 1, 2):
        col = pl.ds(n * wide, wide)
        inner = pl.ds((n % 2) * wide, wide)
        loads[1, n].wait()
        loads[3, n].wait()
        ev[n // 2, :, inner] = ev[n // 2, :, inner] + pg[0, :, col].astype(F32) + pg[2, :, col].astype(F32)
        store = pltpu.make_async_copy(ev.at[n // 2, :, inner], p_out.at[:, col], sems.new())
        store.start()
        stores.append(store)
    for ring in [a_y, a_z, b_y] + list(b_z.values()):
        ring.drain()
    q_copy.wait()
    for store in stores:
        store.wait()


def body(queries, passages, list_owner, list_row, positive, row_weight):
    block, width = queries.shape
    owned = passages.shape[0]
    lanes = list_row.shape[1]
    strip = width // N_NEG
    mid = block // 2
    ids = (list_owner.reshape(1, 1, lanes) * owned + list_row.reshape(1, 1, lanes)).astype(jnp.int32)
    any_space = pl.BlockSpec(memory_space=pl.ANY)
    vmem = pl.BlockSpec(memory_space=pltpu.VMEM)
    wide = width // 4
    scratch = [
        pltpu.VMEM((RING, block, width), BF16),
        pltpu.VMEM((RING, owned, width), BF16),
        pltpu.VMEM((RING, RING, owned, strip), BF16),
        pltpu.VMEM((RING, owned, RING * block), F32),
        pltpu.VMEM((RING, owned, RING * block), BF16),
        pltpu.VMEM((RING, owned, RING * block), BF16),
        pltpu.VMEM((3, owned, width), BF16),
        pltpu.VMEM((4, owned, wide), BF16),
        pltpu.VMEM((2, mid // 2, RING * strip), BF16),
        pltpu.VMEM((2, mid // 2, strip), BF16),
        pltpu.VMEM((2, mid, strip), BF16),
        pltpu.VMEM((RING, 2, mid // 2, strip), BF16),
        pltpu.VMEM((2, mid // 2, strip), BF16),
        pltpu.VMEM((2, mid, strip), BF16),
        pltpu.VMEM((block, strip), BF16),
        pltpu.VMEM((RING * RING, N_NEG, 1, lanes), jnp.int32),
        pltpu.VMEM((lanes, lanes), jnp.int32),
        pltpu.VMEM((RING, owned, lanes), F32),
        pltpu.VMEM((RING, 2, block), F32),
        pltpu.VMEM((RING, 1, RING * block), F32),
        pltpu.VMEM((RING, 1, RING * block), F32),
        pltpu.VMEM((2, RING * block), F32),
        pltpu.VMEM((N_NEG, 2, RING * block), F32),
        pltpu.VMEM((2, RING * block), F32),
        pltpu.VMEM((RING, 2, RING * block), F32),
        pltpu.VMEM((RING, 1, RING * block), F32),
        pltpu.SemaphoreType.DMA((256,)),
    ]
    flops = 6 * RING * block * RING * owned * width
    query_grad, passage_grad, _ = pl.pallas_call(
        kernel,
        out_shape=(
            jax.ShapeDtypeStruct((block, strip), BF16),
            jax.ShapeDtypeStruct((owned, width), F32),
            jax.ShapeDtypeStruct((2, 4, owned, wide), BF16),
        ),
        in_specs=[any_space, any_space, vmem, vmem, vmem],
        out_specs=(any_space, any_space, any_space),
        scratch_shapes=scratch,
        compiler_params=pltpu.CompilerParams(
            collective_id=0, has_side_effects=True, vmem_limit_bytes=60 * 2**20
        ),
        cost_estimate=pl.CostEstimate(flops=flops, bytes_accessed=40 * 2**20, transcendentals=0),
        name="contrastive",
    )(queries, passages, ids, positive.reshape(1, block), row_weight.reshape(1, block))
    return query_grad, passage_grad


def solution(mesh):
    in_specs = (
        P("dp", None),
        P(("dp", "neg"), None),
        P("neg", "dp", None),
        P("neg", "dp"),
        P("dp"),
        P("dp"),
    )
    out_specs = (P("dp", "neg"), P(("dp", "neg"), None))
    return jax.shard_map(body, mesh=mesh, in_specs=in_specs, out_specs=out_specs, check_vma=False)
```

time: 421 us -> 215 us (0.51)
  Pallas kernels: 0 us -> 204 us
  waiting for transfers between devices: 198 us -> 0 us
  blocking collectives: 122 us -> 0 us
  matrix products: 55.1 us -> 0 us
  between operations: 13.9 us -> 0.64 us
  local copies, waits for them, and re-layouts: 18.5 us -> 6.52 us
  other arithmetic: 10.3 us -> 1.19 us
    pallas_call x0 -> x1, Pallas kernels: none -> 204 us  [body(): pl.pallas_call(kernel, out_shape=(jax.ShapeDtypeStruct((block, strip), BF...]
    all_gather x1 -> x0, waiting for transfers between devices: 107 us -> none  [body(): column_block = lax.all_gather(own_rows, 'dp', axis=0, tiled=True)]
    all_to_all x3 -> x0, blocking collectives: 94.7 us -> none  [the longest x1 38.7 us: body(): lax.all_to_all(send_slots.reshape(devices, capacity, width).astype(jnp.bf...]
    reduce_scatter x2 -> x0, waiting for transfers between devices: 90.7 us -> none  [the longest x1 90.7 us: body(): lax.psum_scatter(lax.dot_general(logit_grad, queries, (((0,), (0,)), ((),...]
    dot_general x6 -> x0, matrix products: 55.1 us -> none  [the longest x1 16.5 us: body(): jnp.dot(logit_grad, column_block, preferred_element_type=jnp.float32)]
    psum x1 -> x0, blocking collectives: 14.8 us -> none  [body(): row_total = lax.psum(local_sum * jnp.exp(local_max - row_max), 'neg')]
    pmax x1 -> x0, blocking collectives: 12.7 us -> none  [body(): row_max = lax.pmax(local_max, 'neg')]
    reshape x3 -> x0, local copies, waits for them, and re-layouts: 10.2 us -> none  [the longest x1 4.31 us: body(): returned = returned.reshape(slot_count, width)]
  transfers between devices with their start and end apart: 3 -> 0, of which waited for: 2 -> 0; matrix products, arithmetic and copies ran while one was open for 9% -> 0% of each run, Pallas kernels for 0% -> 0%
where the time goes in v1:
time: 215 us; the launch traced here: 213 us
  Pallas kernels  204 us (95%)
  local copies, waits for them, and re-layouts  6.52 us (3%)
    pallas_call x1, Pallas kernels, body(): pl.pallas_call(kernel, out_shape=(jax.ShapeDtypeStruct((block, strip), BF...  204 us
    unnamed x2, local copies, waits for them, and re-layouts  6.52 us

profile of v1, /device:TPU:1, one launch (start us, length us, event | category | flops | bytes accessed | tf_op | source)
XLA Modules:
  0.0 212.5 jit_solution(5245990974580430760)
XLA Ops:
  0.6 1.2 bitcast_add_fusion.ids_in
  1.8 204.2 %contrastive.1 = (bf16[512,512]{1,0:T(8,128)(2,1)}, f32[256,4096]{1,0:T(8,128)}, bf16[2,4,256,1024]{3,2,1,0:T(8,128)(2,1)}) custom-call(bf16[512,4096]{1,0:T(8,128)(2,1)} %q_in.1, bf16[256,4096]{1,0:T(8,128)(2,1)} %p_in.1, s32[1,1,128]{2,1,0:T(1,128)} %bitcast_add_fusion.ids_in, s32[1,512]{1,0:T(1,128)} %bitcast.6, f32[1,512]{1,0:T(1,128)} %bitcast.7), custom_call_target="tpu_custom_call" | custom-call | flops 51539607552 | bytes 41943040 | tf_op jit(solution)/shard_map/contrastive/pallas_call | solution.py:493
  206.0 1.9 copy.10
  207.9 4.7 %copy.11 = f32[256,4096]{1,0:T(8,128)} copy(f32[256,4096]{1,0:T(8,128)} %get-tuple-element.9) | data formatting | bytes 8388608

commit v2 on v1

v2 whole, which is shorter than its diff:
```python
import math

import jax
import jax.numpy as jnp
from jax import lax
from jax.experimental import pallas as pl
from jax.experimental.pallas import tpu as pltpu
from jax.sharding import PartitionSpec as P

MESH = pl.DeviceIdType.MESH
BF16 = jnp.bfloat16
F32 = jnp.float32
RING = 4
N_NEG = 8
SEMS = 320
LOW = -3.0e38
LOG2E = 1.0 / math.log(2.0)

NN = (((1,), (0,)), ((), ()))
NT = (((1,), (1,)), ((), ()))
TN = (((0,), (0,)), ((), ()))


def dot(a, b, dims):
    return lax.dot_general(a, b, dims, preferred_element_type=F32)


class Sems:
    def __init__(self, ref):
        self.ref = ref
        self.used = 0

    def new(self):
        self.used += 1
        assert self.used <= SEMS
        return self.ref.at[self.used - 1]


class Copy:
    def __init__(self, copy):
        self.copy, self.landed, self.left = copy, False, False
        copy.start()

    def wait_recv(self):
        if not self.landed:
            self.copy.wait_recv()
        self.landed = True

    def wait_send(self):
        if not self.left:
            self.copy.wait_send()
        self.left = True

    def wait(self):
        self.wait_recv()
        self.wait_send()


class RingScatter:
    def __init__(self, send, right, left, view, first, second):
        self.view, self.first, self.second = view, first, second
        self.up, self.down, self.send = right, left, send

    def start(self):
        self.a = self.send(self.view(2, 0), self.first.at[0], self.up)
        self.b = self.send(self.view(2, 1), self.first.at[1], self.down)

    def middle(self):
        self.a.wait_recv()
        self.b.wait_recv()
        part = self.view(1, 0)
        part[...] = (part[...].astype(F32) + self.first[0].astype(F32)).astype(BF16)
        self.c = self.send(self.view(1, None), self.second(0), self.up)
        part = self.view(3, 1)
        part[...] = (part[...].astype(F32) + self.first[1].astype(F32)).astype(BF16)
        self.d = self.send(self.view(3, None), self.second(1), self.down)

    def arrive(self):
        self.c.wait_recv()
        self.d.wait_recv()

    def finish(self):
        self.arrive()
        own = self.view(0, None)
        total = own[...].astype(F32) + self.second(0)[...].astype(F32) + self.second(1)[...].astype(F32)
        own[...] = total.astype(BF16)

    def drain(self):
        for copy in self.copies:
            copy.wait_send()


def kernel(
    q_in, p_in, owner_in, row_in, pos_in, w_in,
    q_own, q_land, p_own, p_land,
    qv, pv, px, ev, gv, gx, pg, pg_first, ay1, az1, bz1, by1,
    ids, table, count, wp, m_b, s_b, st_own, st_in, st_mid, st_y, factor,
    sem_ref,
):
    dp, neg = lax.axis_index("dp"), lax.axis_index("neg")
    x, y = dp // RING, dp % RING
    z, core = neg // 2, neg % 2
    block, width = q_in.shape
    owned = p_in.shape[0]
    strip = width // N_NEG
    scale = 3.0 / math.sqrt(width)
    sems = Sems(sem_ref)

    def device(xx, yy, zz, cc):
        return ((xx % RING) * RING + yy % RING, (zz % RING) * 2 + cc)

    x_peer = [None] + [device(x + k, y, z, core) for k in (1, 2, 3)]
    y_peer = [None] + [device(x, y + k, z, core) for k in (1, 2, 3)]
    z_up, z_down = device(x, y, z + 1, core), device(x, y, z + 3, core)
    other = device(x, y, z, 1 - core)
    n_peer = [None] + [(dp, (neg + k) % N_NEG) for k in range(1, N_NEG)]

    barrier = pltpu.get_barrier_semaphore()
    greeted = x_peer[1:] + y_peer[1:] + n_peer[1:]
    for peer in greeted:
        pl.semaphore_signal(barrier, inc=1, device_id=peer, device_id_type=MESH)
    pl.semaphore_wait(barrier, len(greeted))

    sent = []

    def send(src, dst, to):
        copy = pltpu.make_async_remote_copy(
            src, dst, sems.new(), sems.new(), device_id=to, device_id_type=MESH
        )
        sent.append(Copy(copy))
        return sent[-1]

    half = owned // 2
    lo, hi = pl.ds(0, half), pl.ds(half, half)
    piece = block // 8
    zp = z % 2

    def rows(zz, cc, sub):
        return pl.ds(pl.multiple_of(zz * (4 * piece) + cc * (2 * piece) + sub * piece, piece), piece)

    ids[neg, y, x] = owner_in[...] * owned + row_in[...]
    copies = [send(ids.at[neg, y, x], ids.at[neg, y, x], x_peer[k]) for k in (1, 2, 3)]
    p_right = [send(p_in.at[lo], pv.at[3, lo], x_peer[1])]
    p_left = [send(p_in.at[hi], pv.at[1, hi], x_peer[3])]
    own_q = pltpu.make_async_copy(q_in, qv.at[0], sems.new())
    own_p = pltpu.make_async_copy(p_in, pv.at[0], sems.new())
    own_p.start()
    own_q.start()
    for copy in copies:
        copy.wait_recv()
    copies = [send(ids.at[neg, y], ids.at[neg, y], y_peer[k]) for k in (1, 2, 3)]
    q_right = [send(q_in.at[rows(zp, core, 0)], qv.at[3, rows(zp, core, 0)], y_peer[1])]
    q_left = [send(q_in.at[rows(zp, core, 1)], qv.at[1, rows(zp, core, 1)], y_peer[3])]
    for copy in copies:
        copy.wait_recv()
    copies = [send(ids.at[neg], ids.at[neg], n_peer[k]) for k in range(1, N_NEG)]
    p_right.append(send(p_in.at[hi], pv.at[3, hi], x_peer[1]))
    p_left.append(send(p_in.at[lo], pv.at[1, lo], x_peer[3]))
    q_right.append(send(q_in.at[rows(zp, core, 1)], qv.at[3, rows(zp, core, 1)], y_peer[1]))
    q_left.append(send(q_in.at[rows(zp, core, 0)], qv.at[1, rows(zp, core, 0)], y_peer[3]))
    for copy in copies:
        copy.wait_recv()

    lanes = ids.shape[-1]

    def first_id(b):
        return ((((x + b) % RING) * RING + y) * N_NEG + neg) * owned

    def tally(b):
        name = lax.broadcasted_iota(jnp.int32, (owned, lanes), 0) + first_id(b)

        def more(i, total):
            for j in range(RING * RING):
                total = total + jnp.where(name == ids[i, j // RING, j % RING], 1.0, 0.0)
            return total

        total = lax.fori_loop(0, N_NEG, more, jnp.zeros((owned, lanes), F32))
        listed = dot(total.astype(BF16), jnp.ones((lanes, lanes), BF16), NN)
        count[b] = jnp.where(listed > 0.0, jnp.log(jnp.maximum(listed, 1.0)) * LOG2E, LOW)

    tally(0)

    for i in range(N_NEG):
        for j in range(RING * RING):
            table[pl.ds(i * RING * RING + j, 1), :] = ids[i, j // RING, j % RING]
    pos = pos_in[...]
    entry = jnp.bitwise_and(pos, lanes - 1)
    lister = pos // lanes
    listing = (
        (lister // (RING * RING)) * (RING * RING)
        + jnp.bitwise_and(lister, RING - 1) * RING
        + jnp.bitwise_and(lister // RING, RING - 1)
    )
    side = lax.broadcasted_iota(jnp.int32, (lanes, block), 0)
    chosen = jnp.where(side == listing, 1.0, 0.0).astype(BF16)
    high = (table[...] // 256).astype(F32).astype(BF16)
    low = jnp.bitwise_and(table[...], 255).astype(F32).astype(BF16)
    found = dot(high, chosen, TN) * 256.0 + dot(low, chosen, TN)
    wp[0, 0:1, :] = w_in[...] * scale
    wp[0, 1:2, :] = jnp.sum(jnp.where(side == entry, found, 0.0), axis=0, keepdims=True)
    targets = [send(wp.at[0], wp.at[4 - k], y_peer[k]) for k in (1, 2, 3)]

    def raw(b, r):
        return dot(pv[b], qv[r], NT)

    def finish_logits(b, r, value):
        value = value * (scale * LOG2E) + jnp.concatenate([count[b]] * (block // lanes), axis=1)
        top = jnp.max(value, axis=0, keepdims=True)
        expo = jnp.exp2(value - top)
        place = pl.ds(pl.multiple_of(r * block, block), block)
        coarse = expo.astype(BF16)
        ev[b, 0, :, place] = coarse
        ev[b, 1, :, place] = (expo - coarse.astype(F32)).astype(BF16)
        m_b[b, :, place] = top
        s_b[b, :, place] = jnp.sum(expo, axis=0, keepdims=True)

    def logits(b, r):
        finish_logits(b, r, raw(b, r))

    own_p.wait()
    own_q.wait()
    logits(0, 0)

    from_z, from_core = {}, {}

    def pass_on(r, sub):
        view = qv.at[r, rows(zp, core, sub)]
        from_z[r, sub] = send(view, view, z_up if sub == 0 else z_down)
        from_core[r, 0, sub] = send(view, view, other)

    def pass_over(r, sub):
        from_z[r, sub].wait_recv()
        view = qv.at[r, rows(1 - zp, core, sub)]
        from_core[r, 1, sub] = send(view, view, other)

    def have(r):
        for key in from_core:
            if key[0] == r:
                from_core[key].wait_recv()

    def to_core(b):
        for k in range(RING):
            col = pl.ds(pl.multiple_of((((z + k) % RING) * 2 + 1 - core) * strip, strip), strip)
            crossed.append(send(pv.at[b, :, col], px.at[k, b], other))

    crossed = []
    to_core(0)
    pl.loop(1, RING)(tally)
    q_right[0].wait_recv()
    q_far0 = send(qv.at[3, rows(zp, core, 0)], qv.at[2, rows(zp, core, 0)], y_peer[1])
    pass_on(3, 0)
    q_left[0].wait_recv()
    q_far1 = send(qv.at[1, rows(zp, core, 1)], qv.at[2, rows(zp, core, 1)], y_peer[3])
    pass_on(1, 1)
    p_right[0].wait_recv()
    p_far0 = send(pv.at[3, lo], pv.at[2, lo], x_peer[1])
    p_left[0].wait_recv()
    p_far1 = send(pv.at[1, hi], pv.at[2, hi], x_peer[3])
    q_right[1].wait_recv()
    pass_on(3, 1)
    q_left[1].wait_recv()
    pass_on(1, 0)
    pass_over(3, 0)
    pass_over(1, 1)
    q_far0.wait_recv()
    pass_on(2, 0)
    q_far1.wait_recv()
    pass_on(2, 1)
    pass_over(3, 1)
    pass_over(1, 0)
    have(1)
    have(3)
    pl.loop(0, 2)(lambda j: logits(0, 1 + 2 * j))
    for copy in targets:
        copy.wait_recv()
    p_right[1].wait_recv()
    p_left[1].wait_recv()
    to_core(1)
    to_core(3)

    @pl.loop(0, 6)
    def _(i):
        j = i % 3
        logits(1 + 2 * (i // 3), j + j // 2)

    pass_over(2, 0)
    pass_over(2, 1)
    have(2)
    pl.loop(0, 3)(lambda i: logits(i + i // 2, 2))
    p_far0.wait_recv()
    p_far1.wait_recv()
    to_core(2)
    value = raw(2, 0)
    for r in range(1, RING):
        later = raw(2, r)
        finish_logits(2, r - 1, value)
        value = later
    finish_logits(2, RING - 1, value)

    top = jnp.maximum(jnp.maximum(m_b[0], m_b[1]), jnp.maximum(m_b[2], m_b[3]))
    st_own[0:1, :] = top
    st_own[1:2, :] = sum(s_b[b] * jnp.exp2(m_b[b] - top) for b in range(RING))
    copies = [send(st_own, st_in.at[k], n_peer[k]) for k in range(1, N_NEG)]
    for copy in copies:
        copy.wait_recv()
    for k in range(1, N_NEG):
        top = jnp.maximum(top, st_in[k, 0:1, :])
    mass = st_own[1:2, :] * jnp.exp2(st_own[0:1, :] - top)
    for k in range(1, N_NEG):
        mass = mass + st_in[k, 1:2, :] * jnp.exp2(st_in[k, 0:1, :] - top)
    st_mid[0:1, :] = top
    st_mid[1:2, :] = mass
    copies = [send(st_mid, st_y.at[k], y_peer[k]) for k in (1, 2, 3)]
    for copy in copies:
        copy.wait_recv()
    for r in range(RING):
        mine = pl.ds(r * block, block)
        theirs = [(k, pl.ds(((r + k) % RING) * block, block)) for k in (1, 2, 3)]
        top = st_mid[0:1, mine]
        for k, place in theirs:
            top = jnp.maximum(top, st_y[k, 0:1, place])
        mass = st_mid[1:2, mine] * jnp.exp2(st_mid[0:1, mine] - top)
        for k, place in theirs:
            mass = mass + st_y[k, 1:2, place] * jnp.exp2(st_y[k, 0:1, place] - top)
        weight = wp[r, 0:1, :] / mass
        for b in range(RING):
            factor[b, :, mine] = jnp.exp2(m_b[b, :, mine] - top) * weight

    def gradient(b):
        label = (lax.broadcasted_iota(jnp.int32, (owned, block), 0) + first_id(b)).astype(F32)
        for r in range(RING):
            place = pl.ds(r * block, block)
            hit = jnp.where(label == wp[r, 1:2, :], wp[r, 0:1, :], 0.0)
            expo = ev[b, 0, :, place].astype(F32) + ev[b, 1, :, place].astype(F32)
            gv[b, :, place] = (expo * factor[b, :, place] - hit).astype(BF16)

    wide = width // 4

    def passage_part(b, n):
        col = pl.ds(pl.multiple_of(n * wide, wide), wide)
        return dot(gv[b], qv[:, :, col].reshape(RING * block, wide), NN)

    far = {}
    gradient(2)
    for n in (0, 2, 1, 3):
        col = pl.ds(n * wide, wide)
        pg[1, :, col] = passage_part(2, n).astype(BF16)
        far[n] = send(pg.at[1, :, col], pg_first.at[n], x_peer[1] if n < 2 else x_peer[3])
    grads = [send(gv.at[2], gx.at[2], other)]
    for b in (1, 3, 0):
        gradient(b)
        grads.append(send(gv.at[b], gx.at[b], other))
    for copy in grads + crossed:
        copy.wait_recv()
    for copy in crossed + [p_far0, p_far1]:
        copy.wait_send()

    def query_part(r):
        @pl.loop(0, 2 * RING)
        def _(i):
            k, level = i // 2, i % 2
            place = pl.ds(pl.multiple_of(r * block + level * mid, mid), mid)
            col = pl.ds(pl.multiple_of((((z + k) % RING) * 2 + core) * strip, strip), strip)
            mine = dot(
                gv[:, :, place].reshape(RING * owned, mid),
                pv[:, :, col].reshape(RING * owned, strip),
                TN,
            )
            theirs = dot(
                gx[:, :, place].reshape(RING * owned, mid),
                px[k].reshape(RING * owned, strip),
                TN,
            )
            out = pl.ds(pl.multiple_of(k * strip, strip), strip)
            ev[r, level, :, out] = (mine + theirs).astype(BF16)

    mid = block // 2
    quarter = mid // 2

    def span(part):
        return pl.ds(0, mid) if part is None else pl.ds(part * quarter, quarter)

    def along_y(level, k):
        return lambda rel, part: ev.at[rel, level, span(part), pl.ds(k * strip, strip)]

    def along_z(r, level):
        return lambda rel, part: ev.at[r, level, span(part), pl.ds(rel * strip, strip)]

    def spare(first, k):
        col = pl.ds(pl.multiple_of((2 * k + 1 - core) * strip, strip), strip)
        return lambda way: pv.at[first + way, :, col]

    def landing(level):
        return lambda way: q_land.at[way, pl.ds(level * mid, mid)]

    a_y = [
        RingScatter(send, y_peer[1], y_peer[3], along_y(0, k), ay1.at[k], spare(0, k)) for k in range(RING)
    ]
    b_z = [RingScatter(send, z_up, z_down, along_z(r, 1), bz1.at[r], spare(2, r)) for r in range(RING)]
    a_z = RingScatter(send, z_up, z_down, along_z(0, 0), az1, landing(0))
    b_y = RingScatter(send, y_peer[1], y_peer[3], along_y(1, 0), by1, landing(1))
    order = (2, 1, 3, 0)

    def near_part(b, n):
        col = pl.ds(n * wide, wide)
        value = passage_part(b, n)
        if (b == 1) == (n < 2):
            far[n].wait_recv()
            value = value + pg_first[n].astype(F32)
        pg[b - 1, :, col] = value.astype(BF16)
        send(pg.at[b - 1, :, col], p_land.at[0 if b == 1 else 1, :, col], x_peer[b])

    query_part(2)
    for k in order:
        a_y[k].start()
    b_z[2].start()
    for b, n in ((1, 2), (3, 0), (1, 3), (3, 1)):
        near_part(b, n)
    query_part(1)
    b_z[1].start()
    query_part(3)
    b_z[3].start()
    for k in order:
        a_y[k].middle()
    b_z[2].middle()
    query_part(0)
    b_z[0].start()
    for b, n in ((1, 0), (3, 2), (1, 1), (3, 3)):
        near_part(b, n)
    b_z[1].middle()
    b_z[3].middle()
    b_z[2].finish()
    b_y.start()
    b_z[0].middle()
    for n in range(4):
        far[n].wait_send()
        col = pl.ds(n * wide, wide)
        pg[1, :, col] = passage_part(0, n).astype(BF16)
    p_copy = pltpu.make_async_copy(pg.at[1], p_own, sems.new())
    p_copy.start()
    b_z[1].finish()
    b_z[3].finish()
    a_y[2].finish()
    a_z.start()
    a_y[1].finish()
    a_y[3].finish()
    a_z.middle()
    b_y.middle()
    a_y[0].finish()
    b_z[0].finish()
    upper = pltpu.make_async_copy(along_y(0, 0)(0, None), q_own.at[pl.ds(0, mid)], sems.new())
    lower = pltpu.make_async_copy(along_y(1, 0)(0, None), q_own.at[pl.ds(mid, mid)], sems.new())
    upper.start()
    lower.start()
    for copy in sent:
        copy.wait()
    p_copy.wait()
    upper.wait()
    lower.wait()


def add_up(q_own, q_land, p_own, p_land, q_out, p_out):
    q_out[...] = (q_own[...].astype(F32) + q_land[0].astype(F32) + q_land[1].astype(F32)).astype(BF16)
    p_out[...] = p_own[...].astype(F32) + p_land[0].astype(F32) + p_land[1].astype(F32)


def body(queries, passages, list_owner, list_row, positive, row_weight):
    block, width = queries.shape
    owned = passages.shape[0]
    lanes = list_row.shape[1]
    strip = width // N_NEG
    mid = block // 2
    any_space = pl.BlockSpec(memory_space=pl.ANY)
    vmem = pl.BlockSpec(memory_space=pltpu.VMEM)
    wide = width // 4
    scratch = [
        pltpu.VMEM((RING, block, width), BF16),
        pltpu.VMEM((RING, owned, width), BF16),
        pltpu.VMEM((RING, RING, owned, strip), BF16),
        pltpu.VMEM((RING, 2, owned, RING * block), BF16),
        pltpu.VMEM((RING, owned, RING * block), BF16),
        pltpu.VMEM((RING, owned, RING * block), BF16),
        pltpu.VMEM((3, owned, width), BF16),
        pltpu.VMEM((4, owned, wide), BF16),
        pltpu.VMEM((RING, 2, mid // 2, strip), BF16),
        pltpu.VMEM((2, mid // 2, strip), BF16),
        pltpu.VMEM((RING, 2, mid // 2, strip), BF16),
        pltpu.VMEM((2, mid // 2, strip), BF16),
        pltpu.VMEM((N_NEG, RING, RING, 1, lanes), jnp.int32),
        pltpu.VMEM((lanes, lanes), jnp.int32),
        pltpu.VMEM((RING, owned, lanes), F32),
        pltpu.VMEM((RING, 2, block), F32),
        pltpu.VMEM((RING, 1, RING * block), F32),
        pltpu.VMEM((RING, 1, RING * block), F32),
        pltpu.VMEM((2, RING * block), F32),
        pltpu.VMEM((N_NEG, 2, RING * block), F32),
        pltpu.VMEM((2, RING * block), F32),
        pltpu.VMEM((RING, 2, RING * block), F32),
        pltpu.VMEM((RING, 1, RING * block), F32),
        pltpu.SemaphoreType.DMA((SEMS,)),
    ]
    flops = 6 * RING * block * RING * owned * width
    q_own, q_land, p_own, p_land = pl.pallas_call(
        kernel,
        out_shape=(
            jax.ShapeDtypeStruct((block, strip), BF16),
            jax.ShapeDtypeStruct((2, block, strip), BF16),
            jax.ShapeDtypeStruct((owned, width), BF16),
            jax.ShapeDtypeStruct((2, owned, width), BF16),
        ),
        in_specs=[any_space, any_space, vmem, vmem, vmem, vmem],
        out_specs=(any_space,) * 4,
        scratch_shapes=scratch,
        compiler_params=pltpu.CompilerParams(
            collective_id=0, has_side_effects=True, vmem_limit_bytes=62 * 2**20
        ),
        cost_estimate=pl.CostEstimate(flops=flops, bytes_accessed=40 * 2**20, transcendentals=0),
        name="contrastive",
    )(
        queries,
        passages,
        list_owner.reshape(1, lanes),
        list_row,
        positive.reshape(1, block),
        row_weight.reshape(1, block),
    )
    steps = 4
    q_rows, p_rows = block // steps, owned // steps
    return pl.pallas_call(
        add_up,
        grid=(steps,),
        out_shape=(
            jax.ShapeDtypeStruct((block, strip), BF16),
            jax.ShapeDtypeStruct((owned, width), F32),
        ),
        in_specs=[
            pl.BlockSpec((q_rows, strip), lambda i: (i, 0)),
            pl.BlockSpec((2, q_rows, strip), lambda i: (0, i, 0)),
            pl.BlockSpec((p_rows, width), lambda i: (i, 0)),
            pl.BlockSpec((2, p_rows, width), lambda i: (0, i, 0)),
        ],
        out_specs=(
            pl.BlockSpec((q_rows, strip), lambda i: (i, 0)),
            pl.BlockSpec((p_rows, width), lambda i: (i, 0)),
        ),
        compiler_params=pltpu.CompilerParams(vmem_limit_bytes=32 * 2**20),
        name="add_up",
    )(q_own, q_land, p_own, p_land)


def solution(mesh):
    in_specs = (
        P("dp", None),
        P(("dp", "neg"), None),
        P("neg", "dp", None),
        P("neg", "dp"),
        P("dp"),
        P("dp"),
    )
    out_specs = (P("dp", "neg"), P(("dp", "neg"), None))
    return jax.shard_map(body, mesh=mesh, in_specs=in_specs, out_specs=out_specs, check_vma=False)
```

time: 215 us -> 182 us (0.85); the launches traced: 213 us -> 182 us
  Pallas kernels: 204 us -> 175 us
    pallas_call x1, Pallas kernels: 204 us -> 172 us  [body(): pl.pallas_call(kernel, out_shape=(jax.ShapeDtypeStruct((block, strip), BF...]
    pallas_call x0 -> x1, Pallas kernels: none -> 3.04 us  [body(): pl.pallas_call(add_up, grid=(steps,), out_shape=(jax.ShapeDtypeStruct((bl...]
    unnamed x2 -> x8, local copies, waits for them, and re-layouts: 6.52 us -> 6.04 us
where the time goes in v2:
time: 182 us
  Pallas kernels  175 us (96%)
  local copies, waits for them, and re-layouts  6.04 us (3%)
    pallas_call x1, Pallas kernels, body(): pl.pallas_call(kernel, out_shape=(jax.ShapeDtypeStruct((block, strip), BF...  172 us
    unnamed x8, local copies, waits for them, and re-layouts  6.04 us

profile of v2, /device:TPU:1, one launch (start us, length us, event | category | flops | bytes accessed | tf_op | source)
XLA Modules:
  0.0 182.1 jit_solution(12689663451205810282)
XLA Ops:
  0.6 172.4 %contrastive.1 = (bf16[512,512]{1,0:T(8,128)(2,1)}, bf16[2,512,512]{2,1,0:T(8,128)(2,1)}, bf16[256,4096]{1,0:T(8,128)(2,1)}, bf16[2,256,4096]{2,1,0:T(8,128)(2,1)}) custom-call(bf16[512,4096]{1,0:T(8,128)(2,1)} %q_in.1, bf16[256,4096]{1,0:T(8,128)(2,1)} %p_in.1, s32[1,128]{1,0:T(1,128)} %bitcast.5, s32[1,128]{1,0:T(1,128)} %row_in.1, s32[1,512]{1,0:T(1,128)} %bitcast.3, ...), custom_call_target="tpu_custom_call" | custom-call | flops 51539607552 | bytes 41943040 | tf_op jit(solution)/shard_map/contrastive/pallas_call | solution.py:503
  173.0 0.0 copy-start
  173.0 2.2 %copy-done = bf16[2,256,4096]{2,1,0:T(8,128)(2,1)S(1)} copy-done((bf16[2,256,4096]{2,1,0:T(8,128)(2,1)S(1)}, bf16[2,256,4096]{2,1,0:T(8,128)(2,1)}, u32[]{:S(2)}) %copy-start) | copy-done | bytes 4194328
  175.2 0.0 copy-start.1
  175.2 1.6 copy-done.1
  176.8 0.0 copy-start.2
  176.8 1.2 copy-done.2
  178.0 0.0 copy-start.3
  178.0 1.0 copy-done.3
  179.1 3.0 %add_up.1 = (bf16[512,512]{1,0:T(8,128)(2,1)}, f32[256,4096]{1,0:T(8,128)}) custom-call(bf16[512,512]{1,0:T(8,128)(2,1)S(1)} %copy-done.3, bf16[2,512,512]{2,1,0:T(8,128)(2,1)S(1)} %copy-done.2, bf16[256,4096]{1,0:T(8,128)(2,1)S(1)} %copy-done.1, bf16[2,256,4096]{2,1,0:T(8,128)(2,1)S(1)} %copy-done), custom_call_target="tpu_custom_call" | custom-call | tf_op jit(solution)/shard_map/add_up/pallas_call | solution.py:529
Async XLA Ops:
  173.0 2.2 %copy-start = (bf16[2,256,4096]{2,1,0:T(8,128)(2,1)S(1)}, bf16[2,256,4096]{2,1,0:T(8,128)(2,1)}, u32[]{:S(2)}) copy-start(bf16[2,256,4096]{2,1,0:T(8,128)(2,1)} %get-tuple-element.9.p_land) | copy-start | bytes 12582916
  175.2 1.6 copy-start.1
  176.8 1.2 copy-start.2
  178.0 1.0 copy-start.3

commit v3 on v2

--- a/solution.py
+++ b/solution.py
@@ -12,7 +12,7 @@
 F32 = jnp.float32
 RING = 4
 N_NEG = 8
-SEMS = 320
+SEMS = 400
 LOW = -3.0e38
 LOG2E = 1.0 / math.log(2.0)
 
@@ -290,41 +290,51 @@
     p_far0.wait_recv()
     p_far1.wait_recv()
     to_core(2)
+
+    def merge(pairs):
+        top = pairs[0][0]
+        for m, _ in pairs[1:]:
+            top = jnp.maximum(top, m)
+        return top, sum(mass * jnp.exp2(m - top) for m, mass in pairs)
+
+    def within(r):
+        return pl.ds(r * block, block)
+
+    def share(r):
+        top, mass = merge([(m_b[b, :, within(r)], s_b[b, :, within(r)]) for b in range(RING)])
+        st_own[r, 0:1, :] = top
+        st_own[r, 1:2, :] = mass
+        return [send(st_own.at[r], st_in.at[k, r], n_peer[k]) for k in range(1, N_NEG)]
+
+    def share_on(r):
+        for copy in first_round[r]:
+            copy.wait_recv()
+        refs = [st_own.at[r]] + [st_in.at[k, r] for k in range(1, N_NEG)]
+        top, mass = merge([(ref[0:1, :], ref[1:2, :]) for ref in refs])
+        st_mid[r, 0:1, :] = top
+        st_mid[r, 1:2, :] = mass
+        return [send(st_mid.at[r], st_y.at[k, r], y_peer[k]) for k in (1, 2, 3)]
+
+    first_round, second_round = [], []
     value = raw(2, 0)
     for r in range(1, RING):
         later = raw(2, r)
         finish_logits(2, r - 1, value)
+        first_round.append(share(r - 1))
         value = later
     finish_logits(2, RING - 1, value)
-
-    top = jnp.maximum(jnp.maximum(m_b[0], m_b[1]), jnp.maximum(m_b[2], m_b[3]))
-    st_own[0:1, :] = top
-    st_own[1:2, :] = sum(s_b[b] * jnp.exp2(m_b[b] - top) for b in range(RING))
-    copies = [send(st_own, st_in.at[k], n_peer[k]) for k in range(1, N_NEG)]
-    for copy in copies:
-        copy.wait_recv()
-    for k in range(1, N_NEG):
-        top = jnp.maximum(top, st_in[k, 0:1, :])
-    mass = st_own[1:2, :] * jnp.exp2(st_own[0:1, :] - top)
-    for k in range(1, N_NEG):
-        mass = mass + st_in[k, 1:2, :] * jnp.exp2(st_in[k, 0:1, :] - top)
-    st_mid[0:1, :] = top
-    st_mid[1:2, :] = mass
-    copies = [send(st_mid, st_y.at[k], y_peer[k]) for k in (1, 2, 3)]
-    for copy in copies:
-        copy.wait_recv()
+    first_round.append(share(RING - 1))
     for r in range(RING):
-        mine = pl.ds(r * block, block)
-        theirs = [(k, pl.ds(((r + k) % RING) * block, block)) for k in (1, 2, 3)]
-        top = st_mid[0:1, mine]
-        for k, place in theirs:
-            top = jnp.maximum(top, st_y[k, 0:1, place])
-        mass = st_mid[1:2, mine] * jnp.exp2(st_mid[0:1, mine] - top)
-        for k, place in theirs:
-            mass = mass + st_y[k, 1:2, place] * jnp.exp2(st_y[k, 0:1, place] - top)
+        second_round.append(share_on(r))
+    for copies in second_round:
+        for copy in copies:
+            copy.wait_recv()
+    for r in range(RING):
+        refs = [st_mid.at[r]] + [st_y.at[k, (r + k) % RING] for k in (1, 2, 3)]
+        top, mass = merge([(ref[0:1, :], ref[1:2, :]) for ref in refs])
         weight = wp[r, 0:1, :] / mass
         for b in range(RING):
-            factor[b, :, mine] = jnp.exp2(m_b[b, :, mine] - top) * weight
+            factor[b, :, within(r)] = jnp.exp2(m_b[b, :, within(r)] - top) * weight
 
     def gradient(b):
         label = (lax.broadcasted_iota(jnp.int32, (owned, block), 0) + first_id(b)).astype(F32)
@@ -336,16 +346,16 @@
 
     wide = width // 4
 
-    def passage_part(b, n):
-        col = pl.ds(pl.multiple_of(n * wide, wide), wide)
-        return dot(gv[b], qv[:, :, col].reshape(RING * block, wide), NN)
+    def passage_part(b, col):
+        return dot(gv[b], qv[:, :, col].reshape(RING * block, col.size), NN)
 
     far = {}
     gradient(2)
-    for n in (0, 2, 1, 3):
-        col = pl.ds(n * wide, wide)
-        pg[1, :, col] = passage_part(2, n).astype(BF16)
-        far[n] = send(pg.at[1, :, col], pg_first.at[n], x_peer[1] if n < 2 else x_peer[3])
+    for start, size in ((0, 1), (4, 1), (1, 1), (5, 1), (2, 2), (6, 2)):
+        col = pl.ds(start * strip, size * strip)
+        pg[1, :, col] = passage_part(2, col).astype(BF16)
+        to = x_peer[1] if start < 4 else x_peer[3]
+        far[start] = send(pg.at[1, :, col], pg_first.at[:, col], to)
     grads = [send(gv.at[2], gx.at[2], other)]
     for b in (1, 3, 0):
         gradient(b)
@@ -403,10 +413,12 @@
 
     def near_part(b, n):
         col = pl.ds(n * wide, wide)
-        value = passage_part(b, n)
+        value = passage_part(b, col)
         if (b == 1) == (n < 2):
-            far[n].wait_recv()
-            value = value + pg_first[n].astype(F32)
+            for start in (2 * n, 2 * n + 1):
+                if start in far:
+                    far[start].wait_recv()
+            value = value + pg_first[:, col].astype(F32)
         pg[b - 1, :, col] = value.astype(BF16)
         send(pg.at[b - 1, :, col], p_land.at[0 if b == 1 else 1, :, col], x_peer[b])
 
@@ -416,38 +428,39 @@
     b_z[2].start()
     for b, n in ((1, 2), (3, 0), (1, 3), (3, 1)):
         near_part(b, n)
+    b_z[2].middle()
     query_part(1)
     b_z[1].start()
     query_part(3)
     b_z[3].start()
+    b_z[2].finish()
+    b_y.start()
     for k in order:
         a_y[k].middle()
-    b_z[2].middle()
+    b_z[1].middle()
     query_part(0)
     b_z[0].start()
+    b_z[3].middle()
     for b, n in ((1, 0), (3, 2), (1, 1), (3, 3)):
         near_part(b, n)
-    b_z[1].middle()
-    b_z[3].middle()
-    b_z[2].finish()
-    b_y.start()
+    b_z[1].finish()
     b_z[0].middle()
+    b_z[3].finish()
+    b_y.middle()
+    for copy in far.values():
+        copy.wait_send()
     for n in range(4):
-        far[n].wait_send()
         col = pl.ds(n * wide, wide)
-        pg[1, :, col] = passage_part(0, n).astype(BF16)
+        pg[1, :, col] = passage_part(0, col).astype(BF16)
     p_copy = pltpu.make_async_copy(pg.at[1], p_own, sems.new())
     p_copy.start()
-    b_z[1].finish()
-    b_z[3].finish()
+    b_z[0].finish()
     a_y[2].finish()
     a_z.start()
     a_y[1].finish()
     a_y[3].finish()
     a_z.middle()
-    b_y.middle()
     a_y[0].finish()
-    b_z[0].finish()
     upper = pltpu.make_async_copy(along_y(0, 0)(0, None), q_own.at[pl.ds(0, mid)], sems.new())
     lower = pltpu.make_async_copy(along_y(1, 0)(0, None), q_own.at[pl.ds(mid, mid)], sems.new())
     upper.start()
@@ -481,7 +494,7 @@
         pltpu.VMEM((RING, owned, RING * block), BF16),
         pltpu.VMEM((RING, owned, RING * block), BF16),
         pltpu.VMEM((3, owned, width), BF16),
-        pltpu.VMEM((4, owned, wide), BF16),
+        pltpu.VMEM((owned, width), BF16),
         pltpu.VMEM((RING, 2, mid // 2, strip), BF16),
         pltpu.VMEM((2, mid // 2, strip), BF16),
         pltpu.VMEM((RING, 2, mid // 2, strip), BF16),
@@ -492,10 +505,10 @@
         pltpu.VMEM((RING, 2, block), F32),
         pltpu.VMEM((RING, 1, RING * block), F32),
         pltpu.VMEM((RING, 1, RING * block), F32),
-        pltpu.VMEM((2, RING * block), F32),
-        pltpu.VMEM((N_NEG, 2, RING * block), F32),
-        pltpu.VMEM((2, RING * block), F32),
-        pltpu.VMEM((RING, 2, RING * block), F32),
+        pltpu.VMEM((RING, 2, block), F32),
+        pltpu.VMEM((N_NEG, RING, 2, block), F32),
+        pltpu.VMEM((RING, 2, block), F32),
+        pltpu.VMEM((RING, RING, 2, block), F32),
         pltpu.VMEM((RING, 1, RING * block), F32),
         pltpu.SemaphoreType.DMA((SEMS,)),
     ]
@@ -524,7 +537,7 @@
         positive.reshape(1, block),
         row_weight.reshape(1, block),
     )
-    steps = 4
+    steps = 2
     q_rows, p_rows = block // steps, owned // steps
     return pl.pallas_call(
         add_up,
@@ -543,7 +556,7 @@
             pl.BlockSpec((q_rows, strip), lambda i: (i, 0)),
             pl.BlockSpec((p_rows, width), lambda i: (i, 0)),
         ),
-        compiler_params=pltpu.CompilerParams(vmem_limit_bytes=32 * 2**20),
+        compiler_params=pltpu.CompilerParams(vmem_limit_bytes=60 * 2**20),
         name="add_up",
     )(q_own, q_land, p_own, p_land)
 

time: 182 us -> 175 us (0.962)
  local copies, waits for them, and re-layouts: 6.04 us -> 0 us
    unnamed x8 -> x0, local copies, waits for them, and re-layouts: 6.04 us -> none
    pallas_call x1, Pallas kernels: 172 us -> 169 us  [body(): pl.pallas_call(kernel, out_shape=(jax.ShapeDtypeStruct((block, strip), BF...]
    pallas_call x1, Pallas kernels: 3.04 us -> 5.15 us  [body(): pl.pallas_call(add_up, grid=(steps,), out_shape=(jax.ShapeDtypeStruct((bl...]
where the time goes in v3:
time: 175 us
  Pallas kernels  174 us (99%)
    pallas_call x1, Pallas kernels, body(): pl.pallas_call(kernel, out_shape=(jax.ShapeDtypeStruct((block, strip), BF...  169 us
    pallas_call x1, Pallas kernels, body(): pl.pallas_call(add_up, grid=(steps,), out_shape=(jax.ShapeDtypeStruct((bl...  5.15 us

profile of v3, /device:TPU:1, one launch (start us, length us, event | category | flops | bytes accessed | tf_op | source)
XLA Modules:
  0.0 174.7 jit_solution(10052423027434277279)
XLA Ops:
  0.6 169.0 %contrastive.1 = (bf16[512,512]{1,0:T(8,128)(2,1)}, bf16[2,512,512]{2,1,0:T(8,128)(2,1)}, bf16[256,4096]{1,0:T(8,128)(2,1)}, bf16[2,256,4096]{2,1,0:T(8,128)(2,1)}) custom-call(bf16[512,4096]{1,0:T(8,128)(2,1)} %q_in.1, bf16[256,4096]{1,0:T(8,128)(2,1)} %p_in.1, s32[1,128]{1,0:T(1,128)} %bitcast.5, s32[1,128]{1,0:T(1,128)} %row_in.1, s32[1,512]{1,0:T(1,128)} %bitcast.3, ...), custom_call_target="tpu_custom_call" | custom-call | flops 51539607552 | bytes 41943040 | tf_op jit(solution)/shard_map/contrastive/pallas_call | solution.py:516
  169.6 5.1 %add_up.1 = (bf16[512,512]{1,0:T(8,128)(2,1)}, f32[256,4096]{1,0:T(8,128)}) custom-call(bf16[512,512]{1,0:T(8,128)(2,1)} %get-tuple-element.6.q_own, bf16[2,512,512]{2,1,0:T(8,128)(2,1)} %get-tuple-element.7.q_land, bf16[256,4096]{1,0:T(8,128)(2,1)} %get-tuple-element.8.p_own, bf16[2,256,4096]{2,1,0:T(8,128)(2,1)} %get-tuple-element.9.p_land), custom_call_target="tpu_custom_call" | custom-call | tf_op jit(solution)/shard_map/add_up/pallas_call | solution.py:542

commit v4 on v3

--- a/solution.py
+++ b/solution.py
@@ -447,6 +447,8 @@
     b_z[0].middle()
     b_z[3].finish()
     b_y.middle()
+    a_y[2].finish()
+    a_z.start()
     for copy in far.values():
         copy.wait_send()
     for n in range(4):
@@ -455,8 +457,6 @@
     p_copy = pltpu.make_async_copy(pg.at[1], p_own, sems.new())
     p_copy.start()
     b_z[0].finish()
-    a_y[2].finish()
-    a_z.start()
     a_y[1].finish()
     a_y[3].finish()
     a_z.middle()

time: 175 us -> 172 us (0.983)
  Pallas kernels: 174 us -> 172 us
    pallas_call x1, Pallas kernels: 169 us -> 167 us  [body(): pl.pallas_call(kernel, out_shape=(jax.ShapeDtypeStruct((block, strip), BF...]
where the time goes in v4:
time: 172 us
  Pallas kernels  172 us (100%)
    pallas_call x1, Pallas kernels, body(): pl.pallas_call(kernel, out_shape=(jax.ShapeDtypeStruct((block, strip), BF...  167 us
    pallas_call x1, Pallas kernels, body(): pl.pallas_call(add_up, grid=(steps,), out_shape=(jax.ShapeDtypeStruct((bl...  5.15 us

profile of v4, /device:TPU:1, one launch (start us, length us, event | category | flops | bytes accessed | tf_op | source)
XLA Modules:
  0.0 172.3 jit_solution(5010211640357711971)
XLA Ops:
  0.6 166.5 %contrastive.1 = (bf16[512,512]{1,0:T(8,128)(2,1)}, bf16[2,512,512]{2,1,0:T(8,128)(2,1)}, bf16[256,4096]{1,0:T(8,128)(2,1)}, bf16[2,256,4096]{2,1,0:T(8,128)(2,1)}) custom-call(bf16[512,4096]{1,0:T(8,128)(2,1)} %q_in.1, bf16[256,4096]{1,0:T(8,128)(2,1)} %p_in.1, s32[1,128]{1,0:T(1,128)} %bitcast.5, s32[1,128]{1,0:T(1,128)} %row_in.1, s32[1,512]{1,0:T(1,128)} %bitcast.3, ...), custom_call_target="tpu_custom_call" | custom-call | flops 51539607552 | bytes 41943040 | tf_op jit(solution)/shard_map/contrastive/pallas_call | solution.py:516
  167.2 5.1 %add_up.1 = (bf16[512,512]{1,0:T(8,128)(2,1)}, f32[256,4096]{1,0:T(8,128)}) custom-call(bf16[512,512]{1,0:T(8,128)(2,1)} %get-tuple-element.6.q_own, bf16[2,512,512]{2,1,0:T(8,128)(2,1)} %get-tuple-element.7.q_land, bf16[256,4096]{1,0:T(8,128)(2,1)} %get-tuple-element.8.p_own, bf16[2,256,4096]{2,1,0:T(8,128)(2,1)} %get-tuple-element.9.p_land), custom_call_target="tpu_custom_call" | custom-call | tf_op jit(solution)/shard_map/add_up/pallas_call | solution.py:542

commit v5 on v4

--- a/solution.py
+++ b/solution.py
@@ -94,7 +94,7 @@
     q_in, p_in, owner_in, row_in, pos_in, w_in,
     q_own, q_land, p_own, p_land,
     qv, pv, px, ev, gv, gx, pg, pg_first, ay1, az1, bz1, by1,
-    ids, table, count, wp, m_b, s_b, st_own, st_in, st_mid, st_y, factor,
+    ids, table, count, wp, m_b, s_b, r_b, st_own, st_in, st_mid, st_y, factor,
     sem_ref,
 ):
     dp, neg = lax.axis_index("dp"), lax.axis_index("neg")
@@ -210,7 +210,12 @@
         place = pl.ds(pl.multiple_of(r * block, block), block)
         coarse = expo.astype(BF16)
         ev[b, 0, :, place] = coarse
-        ev[b, 1, :, place] = (expo - coarse.astype(F32)).astype(BF16)
+        rest = expo - coarse.astype(F32)
+        fine = rest.astype(BF16)
+        ev[b, 1, :, place] = fine
+        label = (lax.broadcasted_iota(jnp.int32, (owned, block), 0) + first_id(b)).astype(F32)
+        missed = jnp.where(label == wp[r, 1:2, :], rest - fine.astype(F32), 0.0)
+        r_b[b, :, place] = jnp.sum(missed, axis=0, keepdims=True)
         m_b[b, :, place] = top
         s_b[b, :, place] = jnp.sum(expo, axis=0, keepdims=True)
 
@@ -270,9 +275,9 @@
     pass_over(1, 0)
     have(1)
     have(3)
-    pl.loop(0, 2)(lambda j: logits(0, 1 + 2 * j))
     for copy in targets:
         copy.wait_recv()
+    pl.loop(0, 2)(lambda j: logits(0, 1 + 2 * j))
     p_right[1].wait_recv()
     p_left[1].wait_recv()
     to_core(1)
@@ -340,7 +345,8 @@
         label = (lax.broadcasted_iota(jnp.int32, (owned, block), 0) + first_id(b)).astype(F32)
         for r in range(RING):
             place = pl.ds(r * block, block)
-            hit = jnp.where(label == wp[r, 1:2, :], wp[r, 0:1, :], 0.0)
+            taken = wp[r, 0:1, :] - r_b[b, :, place] * factor[b, :, place]
+            hit = jnp.where(label == wp[r, 1:2, :], taken, 0.0)
             expo = ev[b, 0, :, place].astype(F32) + ev[b, 1, :, place].astype(F32)
             gv[b, :, place] = (expo * factor[b, :, place] - hit).astype(BF16)
 
@@ -503,6 +509,7 @@
         pltpu.VMEM((lanes, lanes), jnp.int32),
         pltpu.VMEM((RING, owned, lanes), F32),
         pltpu.VMEM((RING, 2, block), F32),
+        pltpu.VMEM((RING, 1, RING * block), F32),
         pltpu.VMEM((RING, 1, RING * block), F32),
         pltpu.VMEM((RING, 1, RING * block), F32),
         pltpu.VMEM((RING, 2, block), F32),

time: 172 us -> 173 us (level)
  no operation moved by 1% of the time
where the time goes in v5:
time: 173 us
  Pallas kernels  172 us (99%)
    pallas_call x1, Pallas kernels, body(): pl.pallas_call(kernel, out_shape=(jax.ShapeDtypeStruct((block, strip), BF...  167 us
    pallas_call x1, Pallas kernels, body(): pl.pallas_call(add_up, grid=(steps,), out_shape=(jax.ShapeDtypeStruct((bl...  5.15 us

profile of v5, /device:TPU:1, one launch (start us, length us, event | category | flops | bytes accessed | tf_op | source)
XLA Modules:
  0.0 172.8 jit_solution(10064039018497179403)
XLA Ops:
  0.6 167.0 %contrastive.1 = (bf16[512,512]{1,0:T(8,128)(2,1)}, bf16[2,512,512]{2,1,0:T(8,128)(2,1)}, bf16[256,4096]{1,0:T(8,128)(2,1)}, bf16[2,256,4096]{2,1,0:T(8,128)(2,1)}) custom-call(bf16[512,4096]{1,0:T(8,128)(2,1)} %q_in.1, bf16[256,4096]{1,0:T(8,128)(2,1)} %p_in.1, s32[1,128]{1,0:T(1,128)} %bitcast.5, s32[1,128]{1,0:T(1,128)} %row_in.1, s32[1,512]{1,0:T(1,128)} %bitcast.3, ...), custom_call_target="tpu_custom_call" | custom-call | flops 51539607552 | bytes 41943040 | tf_op jit(solution)/shard_map/contrastive/pallas_call | solution.py:523
  167.6 5.1 %add_up.1 = (bf16[512,512]{1,0:T(8,128)(2,1)}, f32[256,4096]{1,0:T(8,128)}) custom-call(bf16[512,512]{1,0:T(8,128)(2,1)} %get-tuple-element.6.q_own, bf16[2,512,512]{2,1,0:T(8,128)(2,1)} %get-tuple-element.7.q_land, bf16[256,4096]{1,0:T(8,128)(2,1)} %get-tuple-element.8.p_own, bf16[2,256,4096]{2,1,0:T(8,128)(2,1)} %get-tuple-element.9.p_land), custom_call_target="tpu_custom_call" | custom-call | tf_op jit(solution)/shard_map/add_up/pallas_call | solution.py:549
